TPU v7x, 256 devices: a whole 4x4x8 slice. The times are simulated.
256 devices in a mesh: tm: 64 (over x, z, y_hi), patch: 4 (over y_lo, core).
Axes of the slice: x: 4, y: 4 (y_hi: 2, y_lo: 2; y = y_hi * 2 + y_lo), z: 8, core: 2. Of those that a mesh axis runs over, the one named last changes fastest.
Arguments:
- frames_in: bfloat16 [1024, 196, 768], P('tm', 'patch'), may hold values from -12 to 12
- ln_time: float32 [768], replicated, may hold values from 0.25 to 1.75
- w_time_qkv: bfloat16 [768, 2304], replicated, may hold values from -2 to 2
- w_time_out: bfloat16 [768, 768], replicated, may hold values from -0.21875 to 0.21875
- ln_space: float32 [768], replicated, may hold values from 0.25 to 1.75
- w_space_qkv: bfloat16 [768, 2304], replicated, may hold values from -2 to 2
- w_space_out: bfloat16 [768, 768], replicated, may hold values from -0.21875 to 0.21875
- band_lo: int32 [64], P('tm'), may hold values from -1 to 0, as said below
- band_hi: int32 [64], P('tm'), may hold values from 0 to 1, as said below
- valid: int32 [64], replicated, may hold values from 0 to 1, as said below
Outputs:
- frames_out: bfloat16 [1024, 196, 768], P('tm', 'patch')
Inputs may be any that keep to these rules, and one draw needn't show every extreme that they name: `band_lo`: every even-numbered block has -1, and so does block 1; block 3 has 0. `band_hi`: every even-numbered block has 1; block 3 has 0. `valid`: blocks 0 and 1 are 1; block 2 is 0.
All inputs are finite; a program needn't handle non-finite values.
Results may differ from a plain program's by a relative error of at most 0.009.
The roundings to bfloat16 on the way count: a program that leaves them out, or rounds other values in their place, can miss the bound.
Values may be sent and summed in bfloat16 or wider, within the bound.
A program may use at most 128 MiB of HBM per device.

v0:
```python
import functools

import jax
import jax.numpy as jnp
from jax import lax
from jax.experimental import pallas as pl
from jax.experimental.pallas import tpu as pltpu
from jax.sharding import PartitionSpec as P

MESH = pl.DeviceIdType.MESH
F32 = jnp.float32
BF16 = jnp.bfloat16
HEADS = 12
BLOCK = 16
WIDTH = 768
PATCH = 49
HALF = 25
GROUP = 8
CHUNKS = 3
BOUNDS = (0, 9, 17, 25)
TOKENS = 208
VALID = 196
NT = (((1,), (1,)), ((), ()))
NINF = float("-inf")


def dot(a, b):
    return jnp.dot(a, b, preferred_element_type=F32)


def norm_rows(values, gain):
    floats = values.astype(F32)
    center = floats - jnp.mean(floats, axis=-1, keepdims=True)
    spread = jnp.mean(center * center, axis=-1, keepdims=True)
    return (center * lax.rsqrt(spread + 1e-05) * gain).astype(BF16)


def select_matrix(rows, cols, source):
    row = lax.broadcasted_iota(jnp.int32, (rows, cols), 0)
    col = lax.broadcasted_iota(jnp.int32, (rows, cols), 1)
    return jnp.where(source(row) == col, 1.0, 0.0).astype(BF16)


def bits(value, low, count):
    return (value >> low) & ((1 << count) - 1)


def cols_of(j, base=0):
    return pl.ds(pl.multiple_of(base + j * 256, 256), 256)


def kernel(
    x_hbm, wtq_hbm, wto_hbm, wsq_hbm, wso_hbm, gain_t, gain_s, band_lo, band_hi, valid, out,
    wtq, wto, wsq, wso, x4, nrm, kv, qs, mix, snd, lft, recv, rcl, xs, nrm2, qkv, smix,
    om, ol, ret, rl, retl, biasb, bias, perm1, perm2, perm3, perm5,
    lsem, csem, psnd, prcv, osnd, orcv, rsnd, rrcv, bsem,
    ssnd, srcv, lsnd, lrcv, tsnd, trcv, usnd, urcv,
):
    tm = lax.axis_index("tm")
    me = lax.axis_index("patch")
    pairs = lax.axis_size("tm") // 2
    pair = tm // 2
    side = tm % 2
    own = 1 + side
    other = 2 - side
    gid = side * 4 + me
    out_pair = (pair + 2 * side - 1 + pairs) % pairs
    rly_pair = (pair + 1 - 2 * side + pairs) % pairs
    partner = (pair * 2 + 1 - side, me)
    out_dev = (out_pair * 2 + side, me)
    rly_dev = (rly_pair * 2 + side, me)

    def member(k):
        d = (gid + k) % 8
        return d, (pair * 2 + d // 4, d % 4)

    def peer(k):
        s = (me + k) % 4
        return s, (tm, s)

    def remote(src, dst, snd_sem, rcv_sem, device):
        return pltpu.make_async_remote_copy(
            src_ref=src, dst_ref=dst, send_sem=snd_sem, recv_sem=rcv_sem,
            device_id=device, device_id_type=MESH,
        )

    own_copy = pltpu.make_async_copy(x_hbm.at[pl.ds(24 * side, HALF)], x4.at[own], lsem.at[0])
    own_copy.start()
    w_copies = []
    for i, (src, dst) in enumerate(((wtq_hbm, wtq), (wto_hbm, wto), (wsq_hbm, wsq), (wso_hbm, wso))):
        cp = pltpu.make_async_copy(src, dst, lsem.at[1 + i])
        cp.start()
        w_copies.append(cp)

    barrier = pltpu.get_barrier_semaphore()
    for k in range(1, 8):
        pl.semaphore_signal(barrier, inc=1, device_id=member(k)[1], device_id_type=MESH)
    pl.semaphore_signal(barrier, inc=1, device_id=out_dev, device_id_type=MESH)
    pl.semaphore_signal(barrier, inc=1, device_id=rly_dev, device_id_type=MESH)
    pl.semaphore_wait(barrier, 9)

    part, outer = [], []
    for c in range(CHUNKS):
        lo, n = BOUNDS[c], BOUNDS[c + 1] - BOUNDS[c]
        part.append(remote(
            x_hbm.at[pl.ds(24 * (1 - side) + lo, n)], x4.at[own, pl.ds(lo, n)],
            psnd.at[c], prcv.at[c], partner,
        ))
        outer.append(remote(
            x_hbm.at[pl.ds(24 * side + lo, n)], x4.at[3 - 3 * side, pl.ds(lo, n)],
            osnd.at[c], orcv.at[c], out_dev,
        ))
    relay = []
    for c in range(CHUNKS):
        lo, n = BOUNDS[c], BOUNDS[c + 1] - BOUNDS[c]
        relay.append(remote(
            x4.at[other, pl.ds(lo, n)], x4.at[3 * side, pl.ds(lo, n)],
            rsnd.at[c], rrcv.at[c], rly_dev,
        ))
    for c in range(CHUNKS):
        part[c].start()
        outer[c].start()

    left_ok = (band_lo[0] <= -1) & (tm >= 1) & (valid[jnp.maximum(tm - 1, 0)] == 1)
    right_ok = (band_hi[0] >= 1) & (tm <= 2 * pairs - 2) & (valid[jnp.minimum(tm + 1, 2 * pairs - 1)] == 1)
    left = jnp.where(left_ok, 0.0, NINF)
    right = jnp.where(right_ok, 0.0, NINF)
    row8 = lax.broadcasted_iota(jnp.int32, (8, 128), 0)
    biasb[side] = jnp.where(row8 == 0, left, right)
    bias_copy = remote(biasb.at[side], biasb.at[side], bsem.at[0], bsem.at[1], partner)
    bias_copy.start()

    perm1[...] = select_matrix(128, 128, lambda r: (bits(r, 2, 3) << 4) | (bits(r, 5, 2) << 2) | bits(r, 0, 2))
    perm2[...] = select_matrix(
        256, 256,
        lambda r: (bits(r, 3, 1) << 7) | (bits(r, 4, 2) << 5) | (bits(r, 0, 3) << 2) | bits(r, 6, 2),
    )
    perm5[...] = select_matrix(256, 256, lambda r: (bits(r, 0, 4) << 4) | bits(r, 4, 4))
    perm3[0] = select_matrix(
        64, 64, lambda r: jnp.where(bits(r, 0, 4) < 4, (bits(r, 0, 2) << 4) + me * 4 + bits(r, 4, 2), -1)
    )
    perm3[1] = select_matrix(
        64, 64, lambda r: jnp.where(bits(r, 2, 2) == me, (bits(r, 0, 2) << 4) + bits(r, 4, 2), -1)
    )

    lane256 = lax.broadcasted_iota(jnp.int32, (1, 256), 1) >> 6
    head_f = [lane256 == h for h in range(4)]
    head_b = [jnp.where(m, 1.0, 0.0).astype(BF16) for m in head_f]

    bias_copy.wait()
    key_slot = lax.broadcasted_iota(jnp.int32, (32, 64), 1) >> 4
    query_blk = lax.broadcasted_iota(jnp.int32, (32, 64), 0) >> 4
    offset = key_slot - 1 - query_blk
    one = jnp.where(
        query_blk == 0,
        jnp.where(offset < 0, biasb[0, 0:1, 0:64], biasb[0, 1:2, 0:64]),
        jnp.where(offset < 0, biasb[1, 0:1, 0:64], biasb[1, 1:2, 0:64]),
    )
    one = jnp.where(offset == 0, 0.0, one)
    one = jnp.where((offset > 1) | (offset < -1), NINF, one)
    for h in range(4):
        bias[32 * h:32 * h + 32] = one

    def attend(k_rows, q_rows, m_rows):
        q_all = [qs[pl.ds(r, 16)] for r in q_rows]
        for g in range(3):
            cols = slice(256 * g, 256 * g + 256)
            vcols = slice(768 + 256 * g, 768 + 256 * g + 256)
            keys = jnp.concatenate([kv[pl.ds(r, 16), cols] for r in k_rows], axis=0)
            vals = jnp.concatenate([kv[pl.ds(r, 16), vcols] for r in k_rows], axis=0)
            query = jnp.concatenate([q[:, cols] for q in q_all], axis=0)
            stacked = jnp.concatenate([query * m for m in head_b], axis=0)
            score = lax.dot_general(stacked, keys, NT, preferred_element_type=F32) + bias[...]
            raised = jnp.exp(score - jnp.max(score, axis=-1, keepdims=True))
            total = jnp.sum(raised, axis=-1, keepdims=True)
            weight = (raised * (1.0 / total)).astype(BF16)
            mixed = dot(weight, vals)
            picked = jnp.where(head_f[0], mixed[0:32], 0.0)
            for h in range(1, 4):
                picked = jnp.where(head_f[h], mixed[32 * h:32 * h + 32], picked)
            picked = picked.astype(BF16)
            mix[pl.ds(m_rows[0], 16), cols] = picked[:16]
            mix[pl.ds(m_rows[1], 16), cols] = picked[16:]

    lo_at = 24 - 24 * side

    def temporal(c):
        last = c == CHUNKS - 1
        s0 = side + GROUP * c
        main = (0, 128, 256, 416 if last else 384)
        extra = (544, 384, 400, 560)
        rows = 576 if last else 512
        q_rows = 288 if last else 256
        for slot in range(4):
            for half in range(2):
                block = x4[slot, pl.ds(s0 + 4 * half, 4)].reshape(64, WIDTH)
                nrm[main[slot] + 64 * half:main[slot] + 64 * half + 64] = norm_rows(block, gain_t[...])
            if last:
                nrm[extra[slot]:extra[slot] + 16] = norm_rows(x4[slot, lo_at], gain_t[...])

        def kv_tile(j, _):
            kv[0:rows, cols_of(j)] = dot(nrm[0:rows], wtq[:, cols_of(j, WIDTH)]).astype(BF16)
            return 0

        def q_tile(j, _):
            tile = dot(nrm[128:128 + q_rows], wtq[:, cols_of(j)]).astype(BF16)
            qs[0:q_rows, cols_of(j)] = tile * jnp.asarray(0.125, BF16)
            return 0

        lax.fori_loop(0, 6, kv_tile, 0)
        lax.fori_loop(0, 3, q_tile, 0)

        def step(i, _):
            for u in range(2):
                at = pl.multiple_of((2 * i + u) * 16, 16)
                attend([pl.multiple_of(m + at, 16) for m in main],
                       [at, pl.multiple_of(128 + at, 16)], [at, pl.multiple_of(128 + at, 16)])
            return 0

        lax.fori_loop(0, GROUP // 2, step, 0)
        if last:
            attend(list(extra), [256, 272], [256, 272])

        def out_tile(j, _):
            cols = cols_of(j)
            acc = dot(mix[0:q_rows], wto[:, cols])
            base = x4[1:3, pl.ds(s0, GROUP), :, cols].reshape(256, 256)
            after = (base.astype(F32) + acc[0:256]).astype(BF16)
            for b in range(2):
                moved = dot(perm1[...], after[128 * b:128 * b + 128]).astype(BF16)
                snd[c, 4 * b:4 * b + 4, :, cols] = moved.reshape(4, 32, 256)
            if last:
                base = x4[1:3, lo_at, :, cols].reshape(32, 256)
                lft[:, :, cols] = (base.astype(F32) + acc[256:288]).astype(BF16).reshape(2, 16, 256)
            return 0

        lax.fori_loop(0, 3, out_tile, 0)

    def scatter(c):
        copies = []
        pltpu.make_async_copy(snd.at[c, gid], recv.at[c, gid], csem.at[c]).start()
        for k in range(1, 8):
            d, device = member(k)
            cp = remote(snd.at[c, d], recv.at[c, gid], ssnd.at[c, k], srcv.at[c, k], device)
            cp.start()
            copies.append(cp)
        return copies

    own_copy.wait()
    part[0].wait_recv()
    relay[0].start()
    part[1].wait_recv()
    relay[1].start()
    w_copies[0].wait()
    w_copies[1].wait()
    scattered = []
    for c in range(CHUNKS):
        outer[c].wait_recv()
        relay[c].wait_recv()
        temporal(c)
        scattered.append(scatter(c))
        if c == 0:
            part[2].wait_recv()
            relay[2].start()
    left_copies = []
    pltpu.make_async_copy(lft.at[side], rcl.at[me], csem.at[3]).start()
    for k in range(1, 4):
        s, device = peer(k)
        cp = remote(lft.at[side], rcl.at[me], lsnd.at[k], lrcv.at[k], device)
        cp.start()
        left_copies.append(cp)
    w_copies[2].wait()
    w_copies[3].wait()

    def gather(c):
        last = c == CHUNKS - 1
        pltpu.make_async_copy(snd.at[c, gid], recv.at[c, gid], csem.at[c]).wait()
        for cp in scattered[c]:
            cp.wait_recv()
        rows = 320 if last else 256

        def move(j, _):
            cols = cols_of(j)
            moved = dot(perm2[...], recv[c, :, :, cols].reshape(256, 256)).astype(BF16)
            xs[:, 64 * c:64 * c + 64, cols] = moved.reshape(4, 64, 256)
            return 0

        lax.fori_loop(0, 3, move, 0)
        if last:
            pltpu.make_async_copy(lft.at[side], rcl.at[me], csem.at[3]).wait()
            for cp in left_copies:
                cp.wait_recv()

            def move_left(j, _):
                cols = cols_of(j)
                moved = dot(perm3[0], rcl[:, :, cols].reshape(64, 256)).astype(BF16)
                xs[:, 192:208, cols] = moved.reshape(4, 16, 256)
                return 0

            lax.fori_loop(0, 3, move_left, 0)
        for f in range(4):
            nrm2[64 * f:64 * f + 64] = norm_rows(xs[f, 64 * c:64 * c + 64], gain_s[...])
        if last:
            nrm2[256:320] = norm_rows(xs[:, 192:208].reshape(64, WIDTH), gain_s[...])

        def put(tile, cols):
            qkv[:, 64 * c:64 * c + 64, cols] = tile[0:256].reshape(4, 64, 256)
            if last:
                qkv[:, 192:208, cols] = tile[256:320].reshape(4, 16, 256)

        def q_tile(j, _):
            tile = dot(nrm2[0:rows], wsq[:, cols_of(j)]).astype(BF16)
            put(tile * jnp.asarray(0.125, BF16), cols_of(j))
            return 0

        def kv_tile(j, _):
            put(dot(nrm2[0:rows], wsq[:, cols_of(j)]).astype(BF16), cols_of(j))
            return 0

        lax.fori_loop(0, 3, q_tile, 0)
        lax.fori_loop(3, 9, kv_tile, 0)

    for c in range(CHUNKS):
        gather(c)

    lane128 = lax.broadcasted_iota(jnp.int32, (1, 128), 1)
    low = lane128 < 64
    low_b = jnp.where(low, 1.0, 0.0).astype(BF16)
    high_b = jnp.where(low, 0.0, 1.0).astype(BF16)
    key_ok = lax.broadcasted_iota(jnp.int32, (1, TOKENS), 1) < VALID

    def frame(f, _):
        def heads(j, _):
            cols = pl.ds(pl.multiple_of(j * 128, 128), 128)
            query = qkv[f, :, cols]
            keys = qkv[f, :, pl.ds(pl.multiple_of(WIDTH + j * 128, 128), 128)]
            vals = qkv[f, :, pl.ds(pl.multiple_of(2 * WIDTH + j * 128, 128), 128)]
            parts = []
            for mine, rest in ((low_b, high_b), (high_b, low_b)):
                score = lax.dot_general(query * mine, keys, NT, preferred_element_type=F32)
                score = jnp.where(key_ok, score, NINF)
                raised = jnp.exp(score - jnp.max(score, axis=-1, keepdims=True)).astype(BF16)
                parts.append(dot(raised, vals * mine + rest))
            top = jnp.where(low, parts[0], parts[1])
            total = pltpu.roll(jnp.where(low, parts[1], parts[0]), 64, 1)
            smix[:, cols] = (top / total).astype(BF16)
            return 0

        lax.fori_loop(0, 6, heads, 0)

        def out_tile(j, _):
            cols = cols_of(j)
            done = (xs[f, :, cols].astype(F32) + dot(smix[...], wso[:, cols])).astype(BF16)
            om[f, :, :, :, cols] = done[0:192].reshape(3, 4, 16, 256)
            ol[f, :, cols] = done[192:208]
            return 0

        lax.fori_loop(0, 3, out_tile, 0)
        pltpu.make_async_copy(om.at[f, :, me], ret.at[4 * me + f], tsnd.at[f, 0]).start()
        for k in range(1, 4):
            s, device = peer(k)
            remote(om.at[f, :, s], ret.at[4 * me + f], tsnd.at[f, k], trcv.at[f, k], device).start()
        return 0

    lax.fori_loop(0, 4, frame, 0)

    def spread(j, _):
        cols = cols_of(j)
        rl[:, :, cols] = dot(perm3[1], ol[:, :, cols].reshape(64, 256)).astype(BF16).reshape(4, 16, 256)
        return 0

    lax.fori_loop(0, 3, spread, 0)
    pltpu.make_async_copy(rl.at[me], retl.at[me], usnd.at[0]).start()
    for k in range(1, 4):
        s, device = peer(k)
        remote(rl.at[s], retl.at[me], usnd.at[k], urcv.at[k], device).start()

    for f in range(4):
        pltpu.make_async_copy(om.at[f, :, me], ret.at[4 * me + f], tsnd.at[f, 0]).wait()
        for k in range(1, 4):
            s, device = peer(k)
            remote(om.at[f, :, s], ret.at[4 * me + f], tsnd.at[f, k], trcv.at[f, k], device).wait()

    def finish(j, _):
        cols = cols_of(j)
        for c in range(CHUNKS):
            moved = dot(perm5[...], ret[:, c, :, cols].reshape(256, 256)).astype(BF16).reshape(16, 16, 256)
            out[8 * c:8 * c + 8, :, cols] = moved[0:8]
            out[25 + 8 * c:33 + 8 * c, :, cols] = moved[8:16]
        return 0

    lax.fori_loop(0, 3, finish, 0)
    pltpu.make_async_copy(rl.at[me], retl.at[me], usnd.at[0]).wait()
    for k in range(1, 4):
        s, device = peer(k)
        remote(rl.at[s], retl.at[me], usnd.at[k], urcv.at[k], device).wait()
    out[24] = (retl[0] + retl[1]) + (retl[2] + retl[3])

    for c in range(CHUNKS):
        part[c].wait_send()
        outer[c].wait_send()
        relay[c].wait_send()
        for cp in scattered[c]:
            cp.wait_send()
    for cp in left_copies:
        cp.wait_send()


def on_device(frames_in, ln_time, w_time_qkv, w_time_out, ln_space, w_space_qkv, w_space_out, band_lo, band_hi, valid):
    x = jnp.transpose(frames_in, (1, 0, 2))
    any_spec = pl.BlockSpec(memory_space=pl.ANY)
    vmem_spec = pl.BlockSpec(memory_space=pltpu.VMEM)
    smem_spec = pl.BlockSpec(memory_space=pltpu.SMEM)
    dma = pltpu.SemaphoreType.DMA
    scratch = [
        pltpu.VMEM((WIDTH, 3 * WIDTH), BF16),
        pltpu.VMEM((WIDTH, WIDTH), BF16),
        pltpu.VMEM((WIDTH, 3 * WIDTH), BF16),
        pltpu.VMEM((WIDTH, WIDTH), BF16),
        pltpu.VMEM((4, HALF, BLOCK, WIDTH), BF16),
        pltpu.VMEM((576, WIDTH), BF16),
        pltpu.VMEM((576, 2 * WIDTH), BF16),
        pltpu.VMEM((288, WIDTH), BF16),
        pltpu.VMEM((288, WIDTH), BF16),
        pltpu.VMEM((CHUNKS, 8, 32, WIDTH), BF16),
        pltpu.VMEM((2, BLOCK, WIDTH), BF16),
        pltpu.VMEM((CHUNKS, 8, 32, WIDTH), BF16),
        pltpu.VMEM((4, BLOCK, WIDTH), BF16),
        pltpu.VMEM((4, TOKENS, WIDTH), BF16),
        pltpu.VMEM((320, WIDTH), BF16),
        pltpu.VMEM((4, TOKENS, 3 * WIDTH), BF16),
        pltpu.VMEM((TOKENS, WIDTH), BF16),
        pltpu.VMEM((4, CHUNKS, 4, BLOCK, WIDTH), BF16),
        pltpu.VMEM((4, BLOCK, WIDTH), BF16),
        pltpu.VMEM((BLOCK, CHUNKS, BLOCK, WIDTH), BF16),
        pltpu.VMEM((4, BLOCK, WIDTH), BF16),
        pltpu.VMEM((4, BLOCK, WIDTH), BF16),
        pltpu.VMEM((2, 8, 128), F32),
        pltpu.VMEM((128, 64), F32),
        pltpu.VMEM((128, 128), BF16),
        pltpu.VMEM((256, 256), BF16),
        pltpu.VMEM((2, 64, 64), BF16),
        pltpu.VMEM((256, 256), BF16),
        dma((5,)), dma((4,)),
        dma((3,)), dma((3,)), dma((3,)), dma((3,)), dma((3,)), dma((3,)), dma((2,)),
        dma((3, 8)), dma((3, 8)), dma((4,)), dma((4,)),
        dma((4, 4)), dma((4, 4)), dma((4,)), dma((4,)),
    ]
    result = pl.pallas_call(
        kernel,
        out_shape=jax.ShapeDtypeStruct((PATCH, BLOCK, WIDTH), BF16),
        in_specs=[any_spec] * 5 + [vmem_spec] * 2 + [smem_spec] * 3,
        out_specs=vmem_spec,
        scratch_shapes=scratch,
        compiler_params=pltpu.CompilerParams(
            collective_id=0, has_side_effects=True, vmem_limit_bytes=56 * 1024 * 1024
        ),
    )(
        x, w_time_qkv, w_time_out, w_space_qkv, w_space_out,
        ln_time.reshape(1, WIDTH), ln_space.reshape(1, WIDTH), band_lo, band_hi, valid,
    )
    return jnp.transpose(result, (1, 0, 2))


def solution(mesh):
    placed = (P("tm", "patch", None), P(), P(), P(), P(), P(), P(), P("tm"), P("tm"), P())
    return jax.shard_map(
        on_device, mesh=mesh, in_specs=placed, out_specs=P("tm", "patch", None), check_vma=False
    )
```

profile of v0, /device:TPU:1, one launch (start us, length us, event | category | flops | bytes accessed | tf_op | source)
XLA Modules:
  0.0 108.9 jit_solution(2559078559665657163)
XLA Ops:
  1.3 1.3 %reshape.6.gain_t = f32[1,768]{1,0:T(1,128)} reshape(f32[768]{0:T(1024)} %param.11) | data formatting | bytes 6144 | tf_op jit(solution)/shard_map/reshape | solution.py:460
  2.6 1.3 %reshape.7.gain_s = f32[1,768]{1,0:T(1,128)} reshape(f32[768]{0:T(1024)} %param.14) | data formatting | bytes 6144 | tf_op jit(solution)/shard_map/reshape | solution.py:460
  3.8 102.6 %shard_map.100 = bf16[49,16,768]{2,1,0:T(8,128)(2,1)} custom-call(bf16[49,16,768]{2,1,0:T(8,128)(2,1)} %bitcast.3, bf16[768,2304]{1,0:T(8,128)(2,1)} %wtq_hbm.1, bf16[768,768]{1,0:T(8,128)(2,1)} %wto_hbm.1, bf16[768,2304]{1,0:T(8,128)(2,1)} %wsq_hbm.1, bf16[768,768]{1,0:T(8,128)(2,1)} %wso_hbm.1, f32[1,768]{1,0:T(1,128)} %reshape.6.gain_t, ...), custom_call_target="tpu_custom_call" | custom-call | tf_op jit(solution)/shard_map/pallas_call | solution.py:449
  106.5 2.4 %copy.14 = bf16[16,49,768]{2,0,1:T(8,128)(2,1)} copy(bf16[16,49,768]{2,0,1:T(8,128)(2,1)} %bitcast.2) | data formatting | bytes 2408448
where the time goes:
time: 109 us
  Pallas kernels  103 us (94%)
  local copies, waits for them, and re-layouts  4.92 us (5%)
  between operations  1.31 us (1%)
    pallas_call x1, Pallas kernels, on_device(): pl.pallas_call(kernel, out_shape=jax.ShapeDtypeStruct((PATCH, BLOCK, WIDT...  103 us
    unnamed x1, local copies, waits for them, and re-layouts  2.38 us

commit v1 on v0

--- a/solution.py
+++ b/solution.py
@@ -43,10 +43,6 @@
 
 def bits(value, low, count):
     return (value >> low) & ((1 << count) - 1)
-
-
-def cols_of(j, base=0):
-    return pl.ds(pl.multiple_of(base + j * 256, 256), 256)
 
 
 def kernel(
@@ -161,13 +157,26 @@
     for h in range(4):
         bias[32 * h:32 * h + 32] = one
 
-    def attend(k_rows, q_rows, m_rows):
-        q_all = [qs[pl.ds(r, 16)] for r in q_rows]
+    def project(slots, lo, n, queries):
+        rows = 16 * n
+        for i, slot in enumerate(slots):
+            block = x4[slot, lo:lo + n].reshape(rows, WIDTH)
+            nrm[rows * i:rows * i + rows] = norm_rows(block, gain_t[...].reshape(1, WIDTH))
+        normed = nrm[0:rows * len(slots)]
+        pairs_kv = dot(normed, wtq[:, WIDTH:]).astype(BF16)
+        for i, slot in enumerate(slots):
+            kv[slot, 16 * lo:16 * lo + rows] = pairs_kv[rows * i:rows * i + rows]
+        if queries:
+            query = dot(normed, wtq[:, 0:WIDTH]).astype(BF16) * jnp.asarray(0.125, BF16)
+            qs[slots[0] - 1, 16 * lo:16 * lo + rows] = query
+
+    def attend(at, m_rows):
+        q_all = [qs[b, pl.ds(at, 16)] for b in range(2)]
         for g in range(3):
             cols = slice(256 * g, 256 * g + 256)
             vcols = slice(768 + 256 * g, 768 + 256 * g + 256)
-            keys = jnp.concatenate([kv[pl.ds(r, 16), cols] for r in k_rows], axis=0)
-            vals = jnp.concatenate([kv[pl.ds(r, 16), vcols] for r in k_rows], axis=0)
+            keys = jnp.concatenate([kv[slot, pl.ds(at, 16), cols] for slot in range(4)], axis=0)
+            vals = jnp.concatenate([kv[slot, pl.ds(at, 16), vcols] for slot in range(4)], axis=0)
             query = jnp.concatenate([q[:, cols] for q in q_all], axis=0)
             stacked = jnp.concatenate([query * m for m in head_b], axis=0)
             score = lax.dot_general(stacked, keys, NT, preferred_element_type=F32) + bias[...]
@@ -179,62 +188,27 @@
             for h in range(1, 4):
                 picked = jnp.where(head_f[h], mixed[32 * h:32 * h + 32], picked)
             picked = picked.astype(BF16)
-            mix[pl.ds(m_rows[0], 16), cols] = picked[:16]
-            mix[pl.ds(m_rows[1], 16), cols] = picked[16:]
+            mix[m_rows[0]:m_rows[0] + 16, cols] = picked[:16]
+            mix[m_rows[1]:m_rows[1] + 16, cols] = picked[16:]
 
     lo_at = 24 - 24 * side
 
     def temporal(c):
         last = c == CHUNKS - 1
         s0 = side + GROUP * c
-        main = (0, 128, 256, 416 if last else 384)
-        extra = (544, 384, 400, 560)
-        rows = 576 if last else 512
-        q_rows = 288 if last else 256
-        for slot in range(4):
-            for half in range(2):
-                block = x4[slot, pl.ds(s0 + 4 * half, 4)].reshape(64, WIDTH)
-                nrm[main[slot] + 64 * half:main[slot] + 64 * half + 64] = norm_rows(block, gain_t[...])
-            if last:
-                nrm[extra[slot]:extra[slot] + 16] = norm_rows(x4[slot, lo_at], gain_t[...])
-
-        def kv_tile(j, _):
-            kv[0:rows, cols_of(j)] = dot(nrm[0:rows], wtq[:, cols_of(j, WIDTH)]).astype(BF16)
-            return 0
-
-        def q_tile(j, _):
-            tile = dot(nrm[128:128 + q_rows], wtq[:, cols_of(j)]).astype(BF16)
-            qs[0:q_rows, cols_of(j)] = tile * jnp.asarray(0.125, BF16)
-            return 0
-
-        lax.fori_loop(0, 6, kv_tile, 0)
-        lax.fori_loop(0, 3, q_tile, 0)
-
-        def step(i, _):
-            for u in range(2):
-                at = pl.multiple_of((2 * i + u) * 16, 16)
-                attend([pl.multiple_of(m + at, 16) for m in main],
-                       [at, pl.multiple_of(128 + at, 16)], [at, pl.multiple_of(128 + at, 16)])
-            return 0
-
-        lax.fori_loop(0, GROUP // 2, step, 0)
+        for j in range(GROUP):
+            attend(pl.multiple_of((s0 + j) * 16, 16), (16 * j, 128 + 16 * j))
         if last:
-            attend(list(extra), [256, 272], [256, 272])
-
-        def out_tile(j, _):
-            cols = cols_of(j)
-            acc = dot(mix[0:q_rows], wto[:, cols])
-            base = x4[1:3, pl.ds(s0, GROUP), :, cols].reshape(256, 256)
-            after = (base.astype(F32) + acc[0:256]).astype(BF16)
-            for b in range(2):
-                moved = dot(perm1[...], after[128 * b:128 * b + 128]).astype(BF16)
-                snd[c, 4 * b:4 * b + 4, :, cols] = moved.reshape(4, 32, 256)
-            if last:
-                base = x4[1:3, lo_at, :, cols].reshape(32, 256)
-                lft[:, :, cols] = (base.astype(F32) + acc[256:288]).astype(BF16).reshape(2, 16, 256)
-            return 0
-
-        lax.fori_loop(0, 3, out_tile, 0)
+            attend(pl.multiple_of(lo_at * 16, 16), (256, 272))
+        acc = dot(mix[0:288 if last else 256], wto[...])
+        base = x4[1:3, pl.ds(s0, GROUP)].reshape(256, WIDTH)
+        after = (base.astype(F32) + acc[0:256]).astype(BF16)
+        for b in range(2):
+            moved = dot(perm1[...], after[128 * b:128 * b + 128]).astype(BF16)
+            snd[c, 4 * b:4 * b + 4] = moved.reshape(4, 32, WIDTH)
+        if last:
+            base = x4[1:3, lo_at].reshape(32, WIDTH)
+            lft[...] = (base.astype(F32) + acc[256:288]).astype(BF16).reshape(2, 16, WIDTH)
 
     def scatter(c):
         copies = []
@@ -246,22 +220,34 @@
             copies.append(cp)
         return copies
 
+    def span(c):
+        return BOUNDS[c], BOUNDS[c + 1] - BOUNDS[c]
+
+    def project_slot(slot, lo, n):
+        for value in range(2):
+            @pl.when(slot == 1 + value)
+            def _():
+                project((1 + value,), lo, n, True)
+
     own_copy.wait()
-    part[0].wait_recv()
-    relay[0].start()
-    part[1].wait_recv()
-    relay[1].start()
     w_copies[0].wait()
+    project_slot(own, 0, HALF)
+    for c in range(2):
+        part[c].wait_recv()
+        relay[c].start()
+        project_slot(other, *span(c))
     w_copies[1].wait()
     scattered = []
     for c in range(CHUNKS):
         outer[c].wait_recv()
         relay[c].wait_recv()
+        project((0, 3), *span(c), False)
         temporal(c)
         scattered.append(scatter(c))
         if c == 0:
             part[2].wait_recv()
             relay[2].start()
+            project_slot(other, *span(2))
     left_copies = []
     pltpu.make_async_copy(lft.at[side], rcl.at[me], csem.at[3]).start()
     for k in range(1, 4):
@@ -279,46 +265,24 @@
             cp.wait_recv()
         rows = 320 if last else 256
 
-        def move(j, _):
-            cols = cols_of(j)
-            moved = dot(perm2[...], recv[c, :, :, cols].reshape(256, 256)).astype(BF16)
-            xs[:, 64 * c:64 * c + 64, cols] = moved.reshape(4, 64, 256)
-            return 0
-
-        lax.fori_loop(0, 3, move, 0)
+        moved = dot(perm2[...], recv[c].reshape(256, WIDTH)).astype(BF16)
+        xs[:, 64 * c:64 * c + 64] = moved.reshape(4, 64, WIDTH)
+        nrm2[0:256] = norm_rows(moved, gain_s[...].reshape(1, WIDTH))
         if last:
             pltpu.make_async_copy(lft.at[side], rcl.at[me], csem.at[3]).wait()
             for cp in left_copies:
                 cp.wait_recv()
-
-            def move_left(j, _):
-                cols = cols_of(j)
-                moved = dot(perm3[0], rcl[:, :, cols].reshape(64, 256)).astype(BF16)
-                xs[:, 192:208, cols] = moved.reshape(4, 16, 256)
-                return 0
-
-            lax.fori_loop(0, 3, move_left, 0)
-        for f in range(4):
-            nrm2[64 * f:64 * f + 64] = norm_rows(xs[f, 64 * c:64 * c + 64], gain_s[...])
-        if last:
-            nrm2[256:320] = norm_rows(xs[:, 192:208].reshape(64, WIDTH), gain_s[...])
-
-        def put(tile, cols):
-            qkv[:, 64 * c:64 * c + 64, cols] = tile[0:256].reshape(4, 64, 256)
+            moved = dot(perm3[0], rcl[...].reshape(64, WIDTH)).astype(BF16)
+            xs[:, 192:208] = moved.reshape(4, 16, WIDTH)
+            nrm2[256:320] = norm_rows(moved, gain_s[...].reshape(1, WIDTH))
+        for j in range(3):
+            cols = slice(WIDTH * j, WIDTH * j + WIDTH)
+            tile = dot(nrm2[0:rows], wsq[:, cols]).astype(BF16)
+            if j == 0:
+                tile = tile * jnp.asarray(0.125, BF16)
+            qkv[:, 64 * c:64 * c + 64, cols] = tile[0:256].reshape(4, 64, WIDTH)
             if last:
-                qkv[:, 192:208, cols] = tile[256:320].reshape(4, 16, 256)
-
-        def q_tile(j, _):
-            tile = dot(nrm2[0:rows], wsq[:, cols_of(j)]).astype(BF16)
-            put(tile * jnp.asarray(0.125, BF16), cols_of(j))
-            return 0
-
-        def kv_tile(j, _):
-            put(dot(nrm2[0:rows], wsq[:, cols_of(j)]).astype(BF16), cols_of(j))
-            return 0
-
-        lax.fori_loop(0, 3, q_tile, 0)
-        lax.fori_loop(3, 9, kv_tile, 0)
+                qkv[:, 192:208, cols] = tile[256:320].reshape(4, 16, WIDTH)
 
     for c in range(CHUNKS):
         gather(c)
@@ -330,11 +294,11 @@
     key_ok = lax.broadcasted_iota(jnp.int32, (1, TOKENS), 1) < VALID
 
     def frame(f, _):
-        def heads(j, _):
-            cols = pl.ds(pl.multiple_of(j * 128, 128), 128)
+        for j in range(HEADS // 2):
+            cols = slice(128 * j, 128 * j + 128)
             query = qkv[f, :, cols]
-            keys = qkv[f, :, pl.ds(pl.multiple_of(WIDTH + j * 128, 128), 128)]
-            vals = qkv[f, :, pl.ds(pl.multiple_of(2 * WIDTH + j * 128, 128), 128)]
+            keys = qkv[f, :, WIDTH + 128 * j:WIDTH + 128 * j + 128]
+            vals = qkv[f, :, 2 * WIDTH + 128 * j:2 * WIDTH + 128 * j + 128]
             parts = []
             for mine, rest in ((low_b, high_b), (high_b, low_b)):
                 score = lax.dot_general(query * mine, keys, NT, preferred_element_type=F32)
@@ -344,18 +308,9 @@
             top = jnp.where(low, parts[0], parts[1])
             total = pltpu.roll(jnp.where(low, parts[1], parts[0]), 64, 1)
             smix[:, cols] = (top / total).astype(BF16)
-            return 0
-
-        lax.fori_loop(0, 6, heads, 0)
-
-        def out_tile(j, _):
-            cols = cols_of(j)
-            done = (xs[f, :, cols].astype(F32) + dot(smix[...], wso[:, cols])).astype(BF16)
-            om[f, :, :, :, cols] = done[0:192].reshape(3, 4, 16, 256)
-            ol[f, :, cols] = done[192:208]
-            return 0
-
-        lax.fori_loop(0, 3, out_tile, 0)
+        done = (xs[f].astype(F32) + dot(smix[...], wso[...])).astype(BF16)
+        om[f] = done[0:192].reshape(3, 4, 16, WIDTH)
+        ol[f] = done[192:208]
         pltpu.make_async_copy(om.at[f, :, me], ret.at[4 * me + f], tsnd.at[f, 0]).start()
         for k in range(1, 4):
             s, device = peer(k)
@@ -364,12 +319,7 @@
 
     lax.fori_loop(0, 4, frame, 0)
 
-    def spread(j, _):
-        cols = cols_of(j)
-        rl[:, :, cols] = dot(perm3[1], ol[:, :, cols].reshape(64, 256)).astype(BF16).reshape(4, 16, 256)
-        return 0
-
-    lax.fori_loop(0, 3, spread, 0)
+    rl[...] = dot(perm3[1], ol[...].reshape(64, WIDTH)).astype(BF16).reshape(4, 16, WIDTH)
     pltpu.make_async_copy(rl.at[me], retl.at[me], usnd.at[0]).start()
     for k in range(1, 4):
         s, device = peer(k)
@@ -381,15 +331,10 @@
             s, device = peer(k)
             remote(om.at[f, :, s], ret.at[4 * me + f], tsnd.at[f, k], trcv.at[f, k], device).wait()
 
-    def finish(j, _):
-        cols = cols_of(j)
-        for c in range(CHUNKS):
-            moved = dot(perm5[...], ret[:, c, :, cols].reshape(256, 256)).astype(BF16).reshape(16, 16, 256)
-            out[8 * c:8 * c + 8, :, cols] = moved[0:8]
-            out[25 + 8 * c:33 + 8 * c, :, cols] = moved[8:16]
-        return 0
-
-    lax.fori_loop(0, 3, finish, 0)
+    for c in range(CHUNKS):
+        moved = dot(perm5[...], ret[:, c].reshape(256, WIDTH)).astype(BF16).reshape(16, 16, WIDTH)
+        out[8 * c:8 * c + 8] = moved[0:8]
+        out[25 + 8 * c:33 + 8 * c] = moved[8:16]
     pltpu.make_async_copy(rl.at[me], retl.at[me], usnd.at[0]).wait()
     for k in range(1, 4):
         s, device = peer(k)
@@ -418,9 +363,9 @@
         pltpu.VMEM((WIDTH, 3 * WIDTH), BF16),
         pltpu.VMEM((WIDTH, WIDTH), BF16),
         pltpu.VMEM((4, HALF, BLOCK, WIDTH), BF16),
-        pltpu.VMEM((576, WIDTH), BF16),
-        pltpu.VMEM((576, 2 * WIDTH), BF16),
-        pltpu.VMEM((288, WIDTH), BF16),
+        pltpu.VMEM((400, WIDTH), BF16),
+        pltpu.VMEM((4, 400, 2 * WIDTH), BF16),
+        pltpu.VMEM((2, 400, WIDTH), BF16),
         pltpu.VMEM((288, WIDTH), BF16),
         pltpu.VMEM((CHUNKS, 8, 32, WIDTH), BF16),
         pltpu.VMEM((2, BLOCK, WIDTH), BF16),
@@ -457,7 +402,7 @@
         ),
     )(
         x, w_time_qkv, w_time_out, w_space_qkv, w_space_out,
-        ln_time.reshape(1, WIDTH), ln_space.reshape(1, WIDTH), band_lo, band_hi, valid,
+        ln_time, ln_space, band_lo, band_hi, valid,
     )
     return jnp.transpose(result, (1, 0, 2))
 

time: 109 us -> 79.9 us (0.73)
  Pallas kernels: 103 us -> 76 us
  local copies, waits for them, and re-layouts: 4.92 us -> 2.38 us
    pallas_call x1, Pallas kernels: 103 us -> 76 us  [on_device(): pl.pallas_call(kernel, out_shape=jax.ShapeDtypeStruct((PATCH, BLOCK, WIDT...]
    reshape x2 -> x0, local copies, waits for them, and re-layouts: 2.54 us -> none  [the longest x1 1.28 us: on_device(): ln_space.reshape(1, WIDTH)]
where the time goes in v1:
time: 79.9 us; the launch traced here: 79.7 us
  Pallas kernels  76 us (95%)
  local copies, waits for them, and re-layouts  2.38 us (3%)
  between operations  1.31 us (2%)
    pallas_call x1, Pallas kernels, on_device(): pl.pallas_call(kernel, out_shape=jax.ShapeDtypeStruct((PATCH, BLOCK, WIDT...  76 us
    unnamed x1, local copies, waits for them, and re-layouts  2.38 us

profile of v1, /device:TPU:1, one launch (start us, length us, event | category | flops | bytes accessed | tf_op | source)
XLA Modules:
  0.0 79.7 jit_solution(3561742574495597629)
XLA Ops:
  1.3 76.0 %shard_map.100 = bf16[49,16,768]{2,1,0:T(8,128)(2,1)} custom-call(bf16[49,16,768]{2,1,0:T(8,128)(2,1)} %bitcast.3, bf16[768,2304]{1,0:T(8,128)(2,1)} %wtq_hbm.1, bf16[768,768]{1,0:T(8,128)(2,1)} %wto_hbm.1, bf16[768,2304]{1,0:T(8,128)(2,1)} %wsq_hbm.1, bf16[768,768]{1,0:T(8,128)(2,1)} %wso_hbm.1, f32[768]{0:T(1024)} %gain_t.1, f32[768]{0:T(1024)} %gain_s.1, ...), custom_call_target="tpu_custom_call" | custom-call | tf_op jit(solution)/shard_map/pallas_call | solution.py:394
  77.4 2.4 %copy.14 = bf16[16,49,768]{2,0,1:T(8,128)(2,1)} copy(bf16[16,49,768]{2,0,1:T(8,128)(2,1)} %bitcast.2) | data formatting | bytes 2408448

commit v2 on v1

v2 whole, which is shorter than its diff:
```python
import functools

import jax
import jax.numpy as jnp
from jax import lax
from jax.experimental import pallas as pl
from jax.experimental.pallas import tpu as pltpu
from jax.sharding import PartitionSpec as P

MESH = pl.DeviceIdType.MESH
F32 = jnp.float32
BF16 = jnp.bfloat16
HEADS = 12
BLOCK = 16
WIDTH = 768
PATCH = 49
HALF = 25
GROUP = 8
CHUNKS = 3
UNIT = 4
PIECES = 6
UNITS = ((0, 1), (2, 3), (4,), (5,))
BOUNDS = (0, 5, 9, 13, 17, 21, 25)
TOKENS = 208
VALID = 196
NT = (((1,), (1,)), ((), ()))
NINF = float("-inf")


def dot(a, b):
    return jnp.dot(a, b, preferred_element_type=F32)


def norm_rows(values, gain):
    floats = values.astype(F32)
    center = floats - jnp.mean(floats, axis=-1, keepdims=True)
    spread = jnp.mean(center * center, axis=-1, keepdims=True)
    return (center * lax.rsqrt(spread + 1e-05) * gain).astype(BF16)


def select_matrix(rows, cols, source):
    row = lax.broadcasted_iota(jnp.int32, (rows, cols), 0)
    col = lax.broadcasted_iota(jnp.int32, (rows, cols), 1)
    return jnp.where(source(row) == col, 1.0, 0.0).astype(BF16)


def bits(value, low, count):
    return (value >> low) & ((1 << count) - 1)


def kernel(
    x_hbm, wtq_hbm, wto_hbm, wsq_hbm, wso_hbm, gain_t, gain_s, band_lo, band_hi, valid, out,
    wtq, wto, wsq, wso, x4, nrm, kv, qs, mix, snd, lft, recv, rcl, xs, nrm2, qkv, smix,
    om, ol, ret, rl, retl, biasb, bias, perm1, perm2, perm3, perm4, perm5,
    lsem, csem, psnd, prcv, osnd, orcv, rsnd, rrcv, bsem,
    ssnd, srcv, lsnd, lrcv, tsnd, trcv, usnd, urcv,
):
    tm = lax.axis_index("tm")
    me = lax.axis_index("patch")
    pairs = lax.axis_size("tm") // 2
    pair = tm // 2
    side = tm % 2
    own = 1 + side
    other = 2 - side
    gid = side * 4 + me
    out_pair = (pair + 2 * side - 1 + pairs) % pairs
    rly_pair = (pair + 1 - 2 * side + pairs) % pairs
    partner = (pair * 2 + 1 - side, me)
    out_dev = (out_pair * 2 + side, me)
    rly_dev = (rly_pair * 2 + side, me)

    def member(k):
        d = (gid + k) % 8
        return d, (pair * 2 + d // 4, d % 4)

    def peer(k):
        s = (me + k) % 4
        return s, (tm, s)

    def remote(src, dst, snd_sem, rcv_sem, device):
        return pltpu.make_async_remote_copy(
            src_ref=src, dst_ref=dst, send_sem=snd_sem, recv_sem=rcv_sem,
            device_id=device, device_id_type=MESH,
        )

    own_copy = pltpu.make_async_copy(x_hbm.at[pl.ds(24 * side, HALF)], x4.at[own], lsem.at[0])
    own_copy.start()
    w_copies = []
    for i, (src, dst) in enumerate(((wtq_hbm, wtq), (wto_hbm, wto), (wsq_hbm, wsq), (wso_hbm, wso))):
        cp = pltpu.make_async_copy(src, dst, lsem.at[1 + i])
        cp.start()
        w_copies.append(cp)

    left_ok = (band_lo[0] <= -1) & (tm >= 1) & (valid[jnp.maximum(tm - 1, 0)] == 1)
    right_ok = (band_hi[0] >= 1) & (tm <= 2 * pairs - 2) & (valid[jnp.minimum(tm + 1, 2 * pairs - 1)] == 1)
    left = jnp.where(left_ok, 0.0, NINF)
    right = jnp.where(right_ok, 0.0, NINF)
    row8 = lax.broadcasted_iota(jnp.int32, (8, 128), 0)
    biasb[side] = jnp.where(row8 == 0, left, right)

    barrier = pltpu.get_barrier_semaphore()
    for k in range(1, 8):
        pl.semaphore_signal(barrier, inc=1, device_id=member(k)[1], device_id_type=MESH)
    pl.semaphore_signal(barrier, inc=1, device_id=out_dev, device_id_type=MESH)
    pl.semaphore_signal(barrier, inc=1, device_id=rly_dev, device_id_type=MESH)
    pl.semaphore_wait(barrier, 9)

    part, outer = [], []
    for c in range(PIECES):
        lo, n = BOUNDS[c], BOUNDS[c + 1] - BOUNDS[c]
        part.append(remote(
            x_hbm.at[pl.ds(24 * (1 - side) + lo, n)], x4.at[own, pl.ds(lo, n)],
            psnd.at[c], prcv.at[c], partner,
        ))
        outer.append(remote(
            x_hbm.at[pl.ds(24 * side + lo, n)], x4.at[3 - 3 * side, pl.ds(lo, n)],
            osnd.at[c], orcv.at[c], out_dev,
        ))
    relay = []
    for c in range(PIECES):
        lo, n = BOUNDS[c], BOUNDS[c + 1] - BOUNDS[c]
        relay.append(remote(
            x4.at[other, pl.ds(lo, n)], x4.at[3 * side, pl.ds(lo, n)],
            rsnd.at[c], rrcv.at[c], rly_dev,
        ))
    bias_copy = remote(biasb.at[side], biasb.at[side], bsem.at[0], bsem.at[1], partner)
    bias_copy.start()
    for c in range(PIECES):
        part[c].start()
        outer[c].start()

    perm1[...] = select_matrix(
        128, 128,
        lambda r: (bits(r, 6, 1) << 6) | (bits(r, 2, 2) << 4) | (bits(r, 4, 2) << 2) | bits(r, 0, 2),
    )
    perm4[...] = select_matrix(
        128, 128, lambda r: (bits(r, 2, 1) << 6) | (bits(r, 3, 2) << 4) | (bits(r, 0, 2) << 2) | bits(r, 5, 2)
    )
    perm2[...] = select_matrix(
        256, 256,
        lambda r: (bits(r, 3, 1) << 7) | (bits(r, 4, 2) << 5) | (bits(r, 0, 3) << 2) | bits(r, 6, 2),
    )
    perm5[...] = select_matrix(256, 256, lambda r: (bits(r, 0, 4) << 4) | bits(r, 4, 4))
    perm3[0] = select_matrix(
        64, 64, lambda r: jnp.where(bits(r, 0, 4) < 4, (bits(r, 0, 2) << 4) + me * 4 + bits(r, 4, 2), -1)
    )
    perm3[1] = select_matrix(
        64, 64, lambda r: jnp.where(bits(r, 2, 2) == me, (bits(r, 0, 2) << 4) + bits(r, 4, 2), -1)
    )

    lane256 = lax.broadcasted_iota(jnp.int32, (1, 256), 1) >> 6
    head_f = [lane256 == h for h in range(4)]
    head_b = [jnp.where(m, 1.0, 0.0).astype(BF16) for m in head_f]

    def project(slots, lo, n, queries):
        rows = 16 * n
        for i, slot in enumerate(slots):
            block = x4[slot, lo:lo + n].reshape(rows, WIDTH)
            nrm[rows * i:rows * i + rows] = norm_rows(block, gain_t[...].reshape(1, WIDTH))
        normed = nrm[0:rows * len(slots)]
        pairs_kv = dot(normed, wtq[:, WIDTH:]).astype(BF16)
        for i, slot in enumerate(slots):
            kv[slot, 16 * lo:16 * lo + rows] = pairs_kv[rows * i:rows * i + rows]
        if queries:
            query = dot(normed, wtq[:, 0:WIDTH]).astype(BF16) * jnp.asarray(0.125, BF16)
            qs[slots[0] - 1, 16 * lo:16 * lo + rows] = query

    def attend(places):
        scores, values = [], []
        for at, _ in places:
            q_all = [qs[b, pl.ds(at, 16)] for b in range(2)]
            for g in range(3):
                cols = slice(256 * g, 256 * g + 256)
                vcols = slice(768 + 256 * g, 768 + 256 * g + 256)
                keys = jnp.concatenate([kv[slot, pl.ds(at, 16), cols] for slot in range(4)], axis=0)
                values.append(jnp.concatenate([kv[slot, pl.ds(at, 16), vcols] for slot in range(4)], axis=0))
                query = jnp.concatenate([q[:, cols] for q in q_all], axis=0)
                stacked = jnp.concatenate([query * m for m in head_b], axis=0)
                scores.append(lax.dot_general(stacked, keys, NT, preferred_element_type=F32) + bias[...])
        tops = [jnp.max(score, axis=-1, keepdims=True) for score in scores]
        raised = [jnp.exp(score - top) for score, top in zip(scores, tops)]
        scales = [1.0 / jnp.sum(r, axis=-1, keepdims=True) for r in raised]
        weights = [(r * scale).astype(BF16) for r, scale in zip(raised, scales)]
        mixed = [dot(weight, value) for weight, value in zip(weights, values)]
        for i, part_mix in enumerate(mixed):
            rows, cols = places[i // 3][1], slice(256 * (i % 3), 256 * (i % 3) + 256)
            picked = jnp.where(head_f[0], part_mix[0:32], 0.0)
            for h in range(1, 4):
                picked = jnp.where(head_f[h], part_mix[32 * h:32 * h + 32], picked)
            picked = picked.astype(BF16)
            mix[rows[0]:rows[0] + 16, cols] = picked[:16]
            mix[rows[1]:rows[1] + 16, cols] = picked[16:]

    lo_at = 24 - 24 * side

    def temporal(u):
        subs, last = UNITS[u], u == len(UNITS) - 1
        rows = 128 * len(subs)
        places = []
        for i, sub in enumerate(subs):
            for j in range(UNIT):
                at = pl.multiple_of((side + UNIT * sub + j) * 16, 16)
                places.append((at, (128 * i + 16 * j, 128 * i + 64 + 16 * j)))
        if last:
            places.append((pl.multiple_of(lo_at * 16, 16), (rows, rows + 16)))
        attend(places)
        acc = dot(mix[0:rows + 32 if last else rows], wto[...])
        for i, sub in enumerate(subs):
            base = x4[1:3, pl.ds(side + UNIT * sub, UNIT)].reshape(128, WIDTH)
            after = (base.astype(F32) + acc[128 * i:128 * i + 128]).astype(BF16)
            moved = dot(perm1[...], after).astype(BF16)
            half = 16 * (sub % 2)
            snd[sub // 2, :, half:half + 16] = moved.reshape(8, 16, WIDTH)
        if last:
            base = x4[1:3, lo_at].reshape(32, WIDTH)
            lft[...] = (base.astype(F32) + acc[rows:rows + 32]).astype(BF16).reshape(2, 16, WIDTH)

    def lines(u):
        return UNITS[u][0] // 2, pl.ds(16 * (UNITS[u][0] % 2), 16 * len(UNITS[u]))

    def own_piece(u):
        c, rows = lines(u)
        return pltpu.make_async_copy(snd.at[c, gid, rows], recv.at[c, gid, rows], csem.at[u])

    def scatter(u):
        c, rows = lines(u)
        copies = []
        own_piece(u).start()
        for k in (2, 6, 4, 3, 5, 1, 7):
            d, device = member(k)
            cp = remote(snd.at[c, d, rows], recv.at[c, gid, rows], ssnd.at[u, k], srcv.at[u, k], device)
            cp.start()
            copies.append(cp)
        return copies

    def span(first, count):
        return BOUNDS[first], BOUNDS[first + count] - BOUNDS[first]

    def project_slot(slot, lo, n):
        for value in range(2):
            @pl.when(slot == 1 + value)
            def _():
                project((1 + value,), lo, n, True)

    own_copy.wait()
    w_copies[0].wait()
    project_slot(own, 0, HALF)

    bias_copy.wait()
    key_slot = lax.broadcasted_iota(jnp.int32, (32, 64), 1) >> 4
    query_blk = lax.broadcasted_iota(jnp.int32, (32, 64), 0) >> 4
    offset = key_slot - 1 - query_blk
    one = jnp.where(
        query_blk == 0,
        jnp.where(offset < 0, biasb[0, 0:1, 0:64], biasb[0, 1:2, 0:64]),
        jnp.where(offset < 0, biasb[1, 0:1, 0:64], biasb[1, 1:2, 0:64]),
    )
    one = jnp.where(offset == 0, 0.0, one)
    one = jnp.where((offset > 1) | (offset < -1), NINF, one)
    for h in range(4):
        bias[32 * h:32 * h + 32] = one

    w_copies[1].wait()
    scattered = []

    def forward(*pieces):
        for c in pieces:
            part[c].wait_recv()
            relay[c].start()

    def halos(*pieces):
        for c in pieces:
            outer[c].wait_recv()
            relay[c].wait_recv()
        project((0, 3), *span(pieces[0], len(pieces)), False)

    def unit(u):
        temporal(u)
        scattered.append(scatter(u))

    forward(0, 1)
    project_slot(other, *span(0, 2))
    forward(2)
    halos(0, 1)
    forward(3)
    project_slot(other, *span(2, 2))
    unit(0)
    forward(4)
    halos(2, 3)
    forward(5)
    project_slot(other, *span(4, 2))
    unit(1)
    halos(4)
    unit(2)
    halos(5)
    unit(3)
    left_copies = []
    pltpu.make_async_copy(lft.at[side], rcl.at[me], csem.at[len(UNITS)]).start()
    for k in range(1, 4):
        s, device = peer(k)
        cp = remote(lft.at[side], rcl.at[me], lsnd.at[k], lrcv.at[k], device)
        cp.start()
        left_copies.append(cp)
    w_copies[2].wait()
    w_copies[3].wait()

    def gather(u):
        last = u == len(UNITS) - 1
        c, lines_u = lines(u)
        rows = 128 * len(UNITS[u])
        count = rows // 4
        at = 64 * c + 32 * (UNITS[u][0] % 2)
        own_piece(u).wait()
        for cp in scattered[u]:
            cp.wait_recv()
        perm = perm2 if rows == 256 else perm4
        moved = dot(perm[...], recv[c, :, lines_u].reshape(rows, WIDTH)).astype(BF16)
        xs[:, at:at + count] = moved.reshape(4, count, WIDTH)
        nrm2[0:rows] = norm_rows(moved, gain_s[...].reshape(1, WIDTH))
        total = rows
        if last:
            pltpu.make_async_copy(lft.at[side], rcl.at[me], csem.at[len(UNITS)]).wait()
            for cp in left_copies:
                cp.wait_recv()
            moved = dot(perm3[0], rcl[...].reshape(64, WIDTH)).astype(BF16)
            xs[:, 192:208] = moved.reshape(4, 16, WIDTH)
            nrm2[rows:rows + 64] = norm_rows(moved, gain_s[...].reshape(1, WIDTH))
            total = rows + 64
        for j in range(3):
            cols = slice(WIDTH * j, WIDTH * j + WIDTH)
            tile = dot(nrm2[0:total], wsq[:, cols]).astype(BF16)
            if j == 0:
                tile = tile * jnp.asarray(0.125, BF16)
            qkv[:, at:at + count, cols] = tile[0:rows].reshape(4, count, WIDTH)
            if last:
                qkv[:, 192:208, cols] = tile[rows:total].reshape(4, 16, WIDTH)

    for u in range(len(UNITS)):
        gather(u)

    lane128 = lax.broadcasted_iota(jnp.int32, (1, 128), 1)
    low = lane128 < 64
    low_b = jnp.where(low, 1.0, 0.0).astype(BF16)
    high_b = jnp.where(low, 0.0, 1.0).astype(BF16)
    key_ok = lax.broadcasted_iota(jnp.int32, (1, TOKENS), 1) < VALID

    def frame(f, _):
        for first in (0, 3):
            group = range(first, first + 3)
            scores, values = [], []
            for j in group:
                query = qkv[f, :, 128 * j:128 * j + 128]
                keys = qkv[f, :, WIDTH + 128 * j:WIDTH + 128 * j + 128]
                vals = qkv[f, :, 2 * WIDTH + 128 * j:2 * WIDTH + 128 * j + 128]
                for mine, rest in ((low_b, high_b), (high_b, low_b)):
                    score = lax.dot_general(query * mine, keys, NT, preferred_element_type=F32)
                    scores.append(jnp.where(key_ok, score, NINF))
                    values.append(vals * mine + rest)
            tops = [jnp.max(score, axis=-1, keepdims=True) for score in scores]
            raised = [jnp.exp(score - top).astype(BF16) for score, top in zip(scores, tops)]
            parts = [dot(r, value) for r, value in zip(raised, values)]
            for i, j in enumerate(group):
                even, odd = parts[2 * i], parts[2 * i + 1]
                total = pltpu.roll(jnp.where(low, odd, even), 64, 1)
                smix[:, 128 * j:128 * j + 128] = (jnp.where(low, even, odd) / total).astype(BF16)
        done = xs[f].astype(F32) + dot(smix[...], wso[...])
        om[f, 0:2] = done[0:128].astype(BF16).reshape(2, 4, 16, WIDTH)
        halves = [done[128 + 32 * i:160 + 32 * i].reshape(4, 8, WIDTH) for i in range(2)]
        om[f, 2] = jnp.concatenate(halves, axis=1).astype(BF16)
        ol[f] = done[192:208].astype(BF16)
        pltpu.make_async_copy(om.at[f, :, me], ret.at[4 * me + f], tsnd.at[f, 0]).start()
        for k in (2, 1, 3):
            s, device = peer(k)
            remote(om.at[f, :, s], ret.at[4 * me + f], tsnd.at[f, k], trcv.at[f, k], device).start()
        return 0

    lax.fori_loop(0, 4, frame, 0)

    rl[...] = dot(perm3[1], ol[...].reshape(64, WIDTH)).astype(BF16).reshape(4, 16, WIDTH)
    pltpu.make_async_copy(rl.at[me], retl.at[me], usnd.at[0]).start()
    for k in range(1, 4):
        s, device = peer(k)
        remote(rl.at[s], retl.at[me], usnd.at[k], urcv.at[k], device).start()

    for f in range(4):
        pltpu.make_async_copy(om.at[f, :, me], ret.at[4 * me + f], tsnd.at[f, 0]).wait()
        for k in (2, 1, 3):
            s, device = peer(k)
            remote(om.at[f, :, s], ret.at[4 * me + f], tsnd.at[f, k], trcv.at[f, k], device).wait()

    for c in range(CHUNKS):
        moved = dot(perm5[...], ret[:, c].reshape(256, WIDTH)).astype(BF16).reshape(16, 16, WIDTH)
        for i in range(2):
            low_at, high_at = (8 * i, 8 * i + 4) if c == 2 else (4 * i, 4 * i + 8)
            out[8 * c + 4 * i:8 * c + 4 * i + 4] = moved[low_at:low_at + 4]
            out[25 + 8 * c + 4 * i:29 + 8 * c + 4 * i] = moved[high_at:high_at + 4]
    pltpu.make_async_copy(rl.at[me], retl.at[me], usnd.at[0]).wait()
    for k in range(1, 4):
        s, device = peer(k)
        remote(rl.at[s], retl.at[me], usnd.at[k], urcv.at[k], device).wait()
    out[24] = (retl[0] + retl[1]) + (retl[2] + retl[3])

    for c in range(PIECES):
        part[c].wait_send()
        outer[c].wait_send()
        relay[c].wait_send()
    for copies in scattered:
        for cp in copies:
            cp.wait_send()
    for cp in left_copies:
        cp.wait_send()


def on_device(frames_in, ln_time, w_time_qkv, w_time_out, ln_space, w_space_qkv, w_space_out, band_lo, band_hi, valid):
    x = jnp.transpose(frames_in, (1, 0, 2))
    any_spec = pl.BlockSpec(memory_space=pl.ANY)
    vmem_spec = pl.BlockSpec(memory_space=pltpu.VMEM)
    smem_spec = pl.BlockSpec(memory_space=pltpu.SMEM)
    dma = pltpu.SemaphoreType.DMA
    scratch = [
        pltpu.VMEM((WIDTH, 3 * WIDTH), BF16),
        pltpu.VMEM((WIDTH, WIDTH), BF16),
        pltpu.VMEM((WIDTH, 3 * WIDTH), BF16),
        pltpu.VMEM((WIDTH, WIDTH), BF16),
        pltpu.VMEM((4, HALF, BLOCK, WIDTH), BF16),
        pltpu.VMEM((400, WIDTH), BF16),
        pltpu.VMEM((4, 400, 2 * WIDTH), BF16),
        pltpu.VMEM((2, 400, WIDTH), BF16),
        pltpu.VMEM((256, WIDTH), BF16),
        pltpu.VMEM((CHUNKS, 8, 32, WIDTH), BF16),
        pltpu.VMEM((2, BLOCK, WIDTH), BF16),
        pltpu.VMEM((CHUNKS, 8, 32, WIDTH), BF16),
        pltpu.VMEM((4, BLOCK, WIDTH), BF16),
        pltpu.VMEM((4, TOKENS, WIDTH), BF16),
        pltpu.VMEM((320, WIDTH), BF16),
        pltpu.VMEM((4, TOKENS, 3 * WIDTH), BF16),
        pltpu.VMEM((TOKENS, WIDTH), BF16),
        pltpu.VMEM((4, CHUNKS, 4, BLOCK, WIDTH), BF16),
        pltpu.VMEM((4, BLOCK, WIDTH), BF16),
        pltpu.VMEM((BLOCK, CHUNKS, BLOCK, WIDTH), BF16),
        pltpu.VMEM((4, BLOCK, WIDTH), BF16),
        pltpu.VMEM((4, BLOCK, WIDTH), BF16),
        pltpu.VMEM((2, 8, 128), F32),
        pltpu.VMEM((128, 64), F32),
        pltpu.VMEM((128, 128), BF16),
        pltpu.VMEM((256, 256), BF16),
        pltpu.VMEM((2, 64, 64), BF16),
        pltpu.VMEM((128, 128), BF16),
        pltpu.VMEM((256, 256), BF16),
        dma((5,)), dma((len(UNITS) + 1,)),
        *[dma((PIECES,))] * 6, dma((2,)),
        dma((len(UNITS), 8)), dma((len(UNITS), 8)), dma((4,)), dma((4,)),
        dma((4, 4)), dma((4, 4)), dma((4,)), dma((4,)),
    ]
    result = pl.pallas_call(
        kernel,
        out_shape=pltpu.VMEM((PATCH, BLOCK, WIDTH), BF16),
        in_specs=[any_spec] * 5 + [vmem_spec] * 2 + [smem_spec] * 3,
        out_specs=vmem_spec,
        scratch_shapes=scratch,
        compiler_params=pltpu.CompilerParams(
            collective_id=0, has_side_effects=True, vmem_limit_bytes=56 * 1024 * 1024
        ),
    )(
        x, w_time_qkv, w_time_out, w_space_qkv, w_space_out,
        ln_time, ln_space, band_lo, band_hi, valid,
    )
    return jnp.transpose(result, (1, 0, 2))


def solution(mesh):
    placed = (P("tm", "patch", None), P(), P(), P(), P(), P(), P(), P("tm"), P("tm"), P())
    return jax.shard_map(
        on_device, mesh=mesh, in_specs=placed, out_specs=P("tm", "patch", None), check_vma=False
    )
```

time: 79.9 us -> 64.6 us (0.81)
  Pallas kernels: 76 us -> 62.1 us
  local copies, waits for them, and re-layouts: 2.38 us -> 1.02 us
    pallas_call x1, Pallas kernels: 76 us -> 62.1 us  [on_device(): pl.pallas_call(kernel, out_shape=pltpu.VMEM((PATCH, BLOCK, WIDTH), BF16),...]
    unnamed x1, local copies, waits for them, and re-layouts: 2.38 us -> 1.02 us
where the time goes in v2:
time: 64.6 us; the launch traced here: 64.5 us
  Pallas kernels  62.1 us (96%)
  between operations  1.31 us (2%)
  local copies, waits for them, and re-layouts  1.02 us (2%)
    pallas_call x1, Pallas kernels, on_device(): pl.pallas_call(kernel, out_shape=pltpu.VMEM((PATCH, BLOCK, WIDTH), BF16),...  62.1 us

profile of v2, /device:TPU:1, one launch (start us, length us, event | category | flops | bytes accessed | tf_op | source)
XLA Modules:
  0.0 64.5 jit_solution(10570605698768304455)
XLA Ops:
  1.3 62.1 %shard_map.100 = bf16[49,16,768]{2,1,0:T(8,128)(2,1)S(1)} custom-call(bf16[49,16,768]{2,1,0:T(8,128)(2,1)} %bitcast.3, bf16[768,2304]{1,0:T(8,128)(2,1)} %wtq_hbm.1, bf16[768,768]{1,0:T(8,128)(2,1)} %wto_hbm.1, bf16[768,2304]{1,0:T(8,128)(2,1)} %wsq_hbm.1, bf16[768,768]{1,0:T(8,128)(2,1)} %wso_hbm.1, f32[768]{0:T(1024)} %gain_t.1, f32[768]{0:T(1024)} %gain_s.1, ...), custom_call_target="tpu_custom_call" | custom-call | tf_op jit(solution)/shard_map/pallas_call | solution.py:455
  63.4 1.0 %copy.12 = bf16[16,49,768]{2,0,1:T(8,128)(2,1)} copy(bf16[16,49,768]{2,0,1:T(8,128)(2,1)S(1)} %bitcast.2) | data formatting | bytes 2408448

commit v3 on v2

v3 whole, which is shorter than its diff:
```python
import functools

import jax
import jax.numpy as jnp
from jax import lax
from jax.experimental import pallas as pl
from jax.experimental.pallas import tpu as pltpu
from jax.sharding import PartitionSpec as P

MESH = pl.DeviceIdType.MESH
F32 = jnp.float32
BF16 = jnp.bfloat16
HEADS = 12
BLOCK = 16
WIDTH = 768
PATCH = 49
HALF = 25
GROUP = 8
CHUNKS = 3
PIECES = 9
PARCELS = ((0, 0), (0, 16), (1, 0), (1, 16), (2, 0), (2, 16))
BOUNDS = (0, 1, 3, 6, 9, 13, 17, 21, 23, 25)
TOKENS = 208
VALID = 196
NT = (((1,), (1,)), ((), ()))
NINF = float("-inf")


def dot(a, b):
    return jnp.dot(a, b, preferred_element_type=F32)


def norm_rows(values, gain):
    floats = values.astype(F32)
    center = floats - jnp.mean(floats, axis=-1, keepdims=True)
    spread = jnp.mean(center * center, axis=-1, keepdims=True)
    return (center * lax.rsqrt(spread + 1e-05) * gain).astype(BF16)


def select_matrix(rows, cols, source):
    row = lax.broadcasted_iota(jnp.int32, (rows, cols), 0)
    col = lax.broadcasted_iota(jnp.int32, (rows, cols), 1)
    return jnp.where(source(row) == col, 1.0, 0.0).astype(BF16)


def bits(value, low, count):
    return (value >> low) & ((1 << count) - 1)


def kernel(
    x_hbm, wtq_hbm, wto_hbm, wsq_hbm, wso_hbm, gain_t, gain_s, band_lo, band_hi, valid, out,
    wtq, wto, wsq, wso, x4, nrm, kv, qs, mix, snd, lft, recv, rcl, xs, nrm2, qkv, smix,
    om, ol, ret, rl, retl, biasb, bias, perm3, perm6, perm7, perm5,
    lsem, csem, psnd, prcv, rsnd, rrcv, bsem,
    ssnd, srcv, lsnd, lrcv, tsnd, trcv, usnd, urcv,
):
    tm = lax.axis_index("tm")
    me = lax.axis_index("patch")
    pairs = lax.axis_size("tm") // 2
    pair = tm // 2
    side = tm % 2
    own = 1 + side
    gid = side * 4 + me
    home = (me + 2) % 4
    slot_id = side * 4 + home
    partner = (pair * 2 + 1 - side, me)
    before = ((pair - 1 + pairs) % pairs * 2 + side, me)
    behind = ((pair + 1) % pairs * 2 + side, me)

    def member(k):
        d = (gid + k) % 8
        return d, (pair * 2 + d // 4, d % 4)

    def peer(k):
        s = (me + k) % 4
        return s, (tm, s)

    def remote(src, dst, snd_sem, rcv_sem, device):
        return pltpu.make_async_remote_copy(
            src_ref=src, dst_ref=dst, send_sem=snd_sem, recv_sem=rcv_sem,
            device_id=device, device_id_type=MESH,
        )

    w_copies = []
    for i, (src, dst) in enumerate(((wtq_hbm, wtq), (wto_hbm, wto), (wsq_hbm, wsq), (wso_hbm, wso))):
        cp = pltpu.make_async_copy(src, dst, lsem.at[1 + i])
        cp.start()
        w_copies.append(cp)

    left_ok = (band_lo[0] <= -1) & (tm >= 1) & (valid[jnp.maximum(tm - 1, 0)] == 1)
    right_ok = (band_hi[0] >= 1) & (tm <= 2 * pairs - 2) & (valid[jnp.minimum(tm + 1, 2 * pairs - 1)] == 1)
    left = jnp.where(left_ok, 0.0, NINF)
    right = jnp.where(right_ok, 0.0, NINF)
    row8 = lax.broadcasted_iota(jnp.int32, (8, 128), 0)
    biasb[side] = jnp.where(row8 == 0, left, right)

    barrier = pltpu.get_barrier_semaphore()
    for k in range(1, 8):
        pl.semaphore_signal(barrier, inc=1, device_id=member(k)[1], device_id_type=MESH)
    pl.semaphore_signal(barrier, inc=1, device_id=before, device_id_type=MESH)
    pl.semaphore_signal(barrier, inc=1, device_id=behind, device_id_type=MESH)
    pl.semaphore_wait(barrier, 9)

    def piece(c):
        return pl.ds(BOUNDS[c], BOUNDS[c + 1] - BOUNDS[c])

    part, relay = [], []
    for c in range(PIECES):
        lo, n = BOUNDS[c], BOUNDS[c + 1] - BOUNDS[c]
        part.append([
            remote(
                x_hbm.at[pl.ds(25 * half + lo - 1 if c else 24, n)], x4.at[own, piece(c)],
                psnd.at[half, c], prcv.at[side, c], (pair * 2 + half, home),
            )
            for half in range(2)
        ])
        relay.append([
            remote(x4.at[1, piece(c)], x4.at[3, piece(c)], rsnd.at[0, c], rrcv.at[0, c], before),
            remote(x4.at[2, piece(c)], x4.at[0, piece(c)], rsnd.at[1, c], rrcv.at[1, c], behind),
        ])
    bias_copy = remote(biasb.at[side], biasb.at[side], bsem.at[0], bsem.at[1], partner)
    bias_copy.start()
    for c in range(PIECES):
        for cp in part[c]:
            cp.start()

    perm6[...] = select_matrix(
        256, 256,
        lambda r: (bits(r, 7, 1) << 7) | (bits(r, 1, 3) << 4) | (bits(r, 5, 2) << 2)
        | (bits(r, 4, 1) << 1) | bits(r, 0, 1),
    )
    perm7[...] = select_matrix(
        128, 128, lambda r: (bits(r, 3, 1) << 6) | (bits(r, 4, 2) << 4) | (bits(r, 0, 3) << 1) | bits(r, 6, 1)
    )
    perm5[...] = select_matrix(256, 256, lambda r: (bits(r, 0, 4) << 4) | bits(r, 4, 4))
    perm3[0] = select_matrix(
        64, 64, lambda r: jnp.where(bits(r, 0, 4) < 4, (bits(r, 0, 2) << 4) + me * 4 + bits(r, 4, 2), -1)
    )
    perm3[1] = select_matrix(
        64, 64, lambda r: jnp.where(bits(r, 2, 2) == me, (bits(r, 0, 2) << 4) + bits(r, 4, 2), -1)
    )

    lane256 = lax.broadcasted_iota(jnp.int32, (1, 256), 1) >> 6
    head_f = [lane256 == h for h in range(4)]
    head_b = [jnp.where(m, 1.0, 0.0).astype(BF16) for m in head_f]

    def project(slots, lo, n, queries):
        rows = 16 * n
        for i, slot in enumerate(slots):
            block = x4[slot, lo:lo + n].reshape(rows, WIDTH)
            nrm[rows * i:rows * i + rows] = norm_rows(block, gain_t[...].reshape(1, WIDTH))
        normed = nrm[0:rows * len(slots)]
        pairs_kv = dot(normed, wtq[:, WIDTH:]).astype(BF16)
        for i, slot in enumerate(slots):
            kv[slot, 16 * lo:16 * lo + rows] = pairs_kv[rows * i:rows * i + rows]
        if queries:
            query = dot(normed, wtq[:, 0:WIDTH]).astype(BF16) * jnp.asarray(0.125, BF16)
            for i in range(2):
                qs[i, 16 * lo:16 * lo + rows] = query[rows * i:rows * i + rows]

    def attend(places):
        scores, values = [], []
        for at, _ in places:
            q_all = [qs[b, at:at + 16] for b in range(2)]
            for g in range(3):
                cols = slice(256 * g, 256 * g + 256)
                vcols = slice(768 + 256 * g, 768 + 256 * g + 256)
                keys = jnp.concatenate([kv[slot, at:at + 16, cols] for slot in range(4)], axis=0)
                values.append(jnp.concatenate([kv[slot, at:at + 16, vcols] for slot in range(4)], axis=0))
                query = jnp.concatenate([q[:, cols] for q in q_all], axis=0)
                stacked = jnp.concatenate([query * m for m in head_b], axis=0)
                scores.append(lax.dot_general(stacked, keys, NT, preferred_element_type=F32) + bias[...])
        tops = [jnp.max(score, axis=-1, keepdims=True) for score in scores]
        raised = [jnp.exp(score - top) for score, top in zip(scores, tops)]
        scales = [1.0 / jnp.sum(r, axis=-1, keepdims=True) for r in raised]
        weights = [(r * scale).astype(BF16) for r, scale in zip(raised, scales)]
        mixed = [dot(weight, value) for weight, value in zip(weights, values)]
        for i, part_mix in enumerate(mixed):
            rows, cols = places[i // 3][1], slice(256 * (i % 3), 256 * (i % 3) + 256)
            picked = jnp.where(head_f[0], part_mix[0:32], 0.0)
            for h in range(1, 4):
                picked = jnp.where(head_f[h], part_mix[32 * h:32 * h + 32], picked)
            picked = picked.astype(BF16)
            mix[rows[0]:rows[0] + 16, cols] = picked[:16]
            mix[rows[1]:rows[1] + 16, cols] = picked[16:]

    def mix_unit(u):
        places = [(16 * (1 + GROUP * u + j), (16 * j, 128 + 16 * j)) for j in range(GROUP)]
        attend(places + [(0, (256, 272))] if u == 0 else places)

    def send_unit(u):
        first = 1 + GROUP * u
        acc = dot(mix[0:288 if u == 0 else 256], wto[...])
        base = x4[1:3, first:first + GROUP].reshape(256, WIDTH)
        after = (base.astype(F32) + acc[0:256]).astype(BF16)
        snd[u] = dot(perm6[...], after).astype(BF16).reshape(8, 32, WIDTH)
        if u == 0:
            base = x4[1:3, 0].reshape(32, WIDTH)
            lft[...] = (base.astype(F32) + acc[256:288]).astype(BF16).reshape(2, 16, WIDTH)
        scatter(2 * u)

    def own_piece(p):
        c, at = PARCELS[p]
        rows = pl.ds(at, 16)
        return pltpu.make_async_copy(snd.at[c, gid, rows], recv.at[c, slot_id, rows], csem.at[p])

    scattered = {}

    def scatter(p):
        c, at = PARCELS[p]
        rows = pl.ds(at, 16)
        scattered[p] = []
        own_piece(p).start()
        for k in (2, 6, 4, 3, 5, 1, 7):
            d, device = member(k)
            cp = remote(snd.at[c, d, rows], recv.at[c, slot_id, rows], ssnd.at[p, k], srcv.at[p, k], device)
            cp.start()
            scattered[p].append(cp)

    def span(first, count):
        return BOUNDS[first], BOUNDS[first + count] - BOUNDS[first]

    bias_copy.wait()
    key_slot = lax.broadcasted_iota(jnp.int32, (32, 64), 1) >> 4
    query_blk = lax.broadcasted_iota(jnp.int32, (32, 64), 0) >> 4
    offset = key_slot - 1 - query_blk
    one = jnp.where(
        query_blk == 0,
        jnp.where(offset < 0, biasb[0, 0:1, 0:64], biasb[0, 1:2, 0:64]),
        jnp.where(offset < 0, biasb[1, 0:1, 0:64], biasb[1, 1:2, 0:64]),
    )
    one = jnp.where(offset == 0, 0.0, one)
    one = jnp.where((offset > 1) | (offset < -1), NINF, one)
    for h in range(4):
        bias[32 * h:32 * h + 32] = one

    w_copies[0].wait()
    w_copies[1].wait()

    def forward(c):
        for b in range(2):
            remote(
                x4.at[1 + b, piece(c)], x4.at[1 + b, piece(c)], psnd.at[b, c], prcv.at[b, c], partner
            ).wait_recv()
            relay[c][b].start()

    def mine(*pieces):
        project((1, 2), *span(pieces[0], len(pieces)), True)

    def halos(*pieces):
        for c in pieces:
            for cp in relay[c]:
                cp.wait_recv()

    def beside(*pieces):
        project((0, 3), *span(pieces[0], len(pieces)), False)

    for c in range(4):
        forward(c)
    mine(0, 1, 2, 3)
    forward(4)
    mine(4)
    halos(0, 1, 2, 3)
    forward(5)
    beside(0, 1, 2, 3)
    mix_unit(0)
    forward(6)
    send_unit(0)
    left_copies = []
    pltpu.make_async_copy(lft.at[side], rcl.at[home], csem.at[len(PARCELS)]).start()
    for k in range(1, 4):
        s, device = peer(k)
        cp = remote(lft.at[side], rcl.at[home], lsnd.at[k], lrcv.at[k], device)
        cp.start()
        left_copies.append(cp)
    forward(7)
    mine(5, 6)
    forward(8)
    halos(4, 5)
    beside(4, 5)
    mix_unit(1)
    send_unit(1)
    mine(7, 8)
    halos(6, 7, 8)
    beside(6, 7, 8)
    mix_unit(2)
    send_unit(2)
    for p in (1, 3, 5):
        scatter(p)
    w_copies[2].wait()
    w_copies[3].wait()

    def gather(p):
        c, first = PARCELS[p]
        last, at = p == 0, 64 * c
        frames = slice(first // 8, first // 8 + 2)
        own_piece(p).wait()
        for cp in scattered[p]:
            cp.wait_recv()
        moved = dot(perm7[...], recv[c, :, first:first + 16].reshape(128, WIDTH)).astype(BF16)
        xs[frames, at:at + 64] = moved.reshape(2, 64, WIDTH)
        nrm2[0:128] = norm_rows(moved, gain_s[...].reshape(1, WIDTH))
        total = 128
        if last:
            pltpu.make_async_copy(lft.at[side], rcl.at[home], csem.at[len(PARCELS)]).wait()
            for cp in left_copies:
                cp.wait_recv()
            moved = dot(perm3[0], rcl[...].reshape(64, WIDTH)).astype(BF16)
            xs[:, 192:208] = moved.reshape(4, 16, WIDTH)
            nrm2[128:192] = norm_rows(moved, gain_s[...].reshape(1, WIDTH))
            total = 192
        for j in range(3):
            cols = slice(WIDTH * j, WIDTH * j + WIDTH)
            tile = dot(nrm2[0:total], wsq[:, cols]).astype(BF16)
            if j == 0:
                tile = tile * jnp.asarray(0.125, BF16)
            qkv[frames, at:at + 64, cols] = tile[0:128].reshape(2, 64, WIDTH)
            if last:
                qkv[:, 192:208, cols] = tile[128:192].reshape(4, 16, WIDTH)

    lane128 = lax.broadcasted_iota(jnp.int32, (1, 128), 1)
    low = lane128 < 64
    low_b = jnp.where(low, 1.0, 0.0).astype(BF16)
    high_b = jnp.where(low, 0.0, 1.0).astype(BF16)
    key_ok = lax.broadcasted_iota(jnp.int32, (1, TOKENS), 1) < VALID

    def frame(f, _):
        for first in (0, 3):
            group = range(first, first + 3)
            scores, values = [], []
            for j in group:
                query = qkv[f, :, 128 * j:128 * j + 128]
                keys = qkv[f, :, WIDTH + 128 * j:WIDTH + 128 * j + 128]
                vals = qkv[f, :, 2 * WIDTH + 128 * j:2 * WIDTH + 128 * j + 128]
                for mine, rest in ((low_b, high_b), (high_b, low_b)):
                    score = lax.dot_general(query * mine, keys, NT, preferred_element_type=F32)
                    scores.append(jnp.where(key_ok, score, NINF))
                    values.append(vals * mine + rest)
            tops = [jnp.max(score, axis=-1, keepdims=True) for score in scores]
            raised = [jnp.exp(score - top).astype(BF16) for score, top in zip(scores, tops)]
            parts = [dot(r, value) for r, value in zip(raised, values)]
            for i, j in enumerate(group):
                even, odd = parts[2 * i], parts[2 * i + 1]
                total = pltpu.roll(jnp.where(low, odd, even), 64, 1)
                smix[:, 128 * j:128 * j + 128] = (jnp.where(low, even, odd) / total).astype(BF16)
        done = xs[f].astype(F32) + dot(smix[...], wso[...])
        om[f] = done[0:192].astype(BF16).reshape(3, 4, 16, WIDTH)
        ol[f] = done[192:208].astype(BF16)
        pltpu.make_async_copy(om.at[f, :, me], ret.at[4 * me + f], tsnd.at[f, 0]).start()
        for k in (2, 1, 3):
            s, device = peer(k)
            remote(om.at[f, :, s], ret.at[4 * me + f], tsnd.at[f, k], trcv.at[f, k], device).start()
        return 0

    for c in range(PIECES):
        for cp in part[c] + relay[c]:
            cp.wait_send()
    for p in (0, 2, 4):
        gather(p)
    lax.fori_loop(0, 2, frame, 0)
    for p in (1, 3, 5):
        gather(p)
    lax.fori_loop(2, 4, frame, 0)
    for copies in scattered.values():
        for cp in copies:
            cp.wait_send()
    for cp in left_copies:
        cp.wait_send()

    rl[...] = dot(perm3[1], ol[...].reshape(64, WIDTH)).astype(BF16).reshape(4, 16, WIDTH)
    pltpu.make_async_copy(rl.at[me], retl.at[me], usnd.at[0]).start()
    for k in range(1, 4):
        s, device = peer(k)
        remote(rl.at[s], retl.at[me], usnd.at[k], urcv.at[k], device).start()

    for f in range(4):
        pltpu.make_async_copy(om.at[f, :, me], ret.at[4 * me + f], tsnd.at[f, 0]).wait()
        for k in (2, 1, 3):
            s, device = peer(k)
            remote(om.at[f, :, s], ret.at[4 * me + f], tsnd.at[f, k], trcv.at[f, k], device).wait()

    for c in range(CHUNKS):
        moved = dot(perm5[...], ret[:, c].reshape(256, WIDTH)).astype(BF16).reshape(16, 16, WIDTH)
        out[8 * c:8 * c + 8] = moved[0:8]
        out[25 + 8 * c:33 + 8 * c] = moved[8:16]
    pltpu.make_async_copy(rl.at[me], retl.at[me], usnd.at[0]).wait()
    for k in range(1, 4):
        s, device = peer(k)
        remote(rl.at[s], retl.at[me], usnd.at[k], urcv.at[k], device).wait()
    out[24] = (retl[0] + retl[1]) + (retl[2] + retl[3])


def on_device(frames_in, ln_time, w_time_qkv, w_time_out, ln_space, w_space_qkv, w_space_out, band_lo, band_hi, valid):
    x = jnp.transpose(frames_in, (1, 0, 2))
    any_spec = pl.BlockSpec(memory_space=pl.ANY)
    vmem_spec = pl.BlockSpec(memory_space=pltpu.VMEM)
    smem_spec = pl.BlockSpec(memory_space=pltpu.SMEM)
    dma = pltpu.SemaphoreType.DMA
    scratch = [
        pltpu.VMEM((WIDTH, 3 * WIDTH), BF16),
        pltpu.VMEM((WIDTH, WIDTH), BF16),
        pltpu.VMEM((WIDTH, 3 * WIDTH), BF16),
        pltpu.VMEM((WIDTH, WIDTH), BF16),
        pltpu.VMEM((4, HALF, BLOCK, WIDTH), BF16),
        pltpu.VMEM((288, WIDTH), BF16),
        pltpu.VMEM((4, 400, 2 * WIDTH), BF16),
        pltpu.VMEM((2, 400, WIDTH), BF16),
        pltpu.VMEM((288, WIDTH), BF16),
        pltpu.VMEM((CHUNKS, 8, 32, WIDTH), BF16),
        pltpu.VMEM((2, BLOCK, WIDTH), BF16),
        pltpu.VMEM((CHUNKS, 8, 32, WIDTH), BF16),
        pltpu.VMEM((4, BLOCK, WIDTH), BF16),
        pltpu.VMEM((4, TOKENS, WIDTH), BF16),
        pltpu.VMEM((192, WIDTH), BF16),
        pltpu.VMEM((4, TOKENS, 3 * WIDTH), BF16),
        pltpu.VMEM((TOKENS, WIDTH), BF16),
        pltpu.VMEM((4, CHUNKS, 4, BLOCK, WIDTH), BF16),
        pltpu.VMEM((4, BLOCK, WIDTH), BF16),
        pltpu.VMEM((BLOCK, CHUNKS, BLOCK, WIDTH), BF16),
        pltpu.VMEM((4, BLOCK, WIDTH), BF16),
        pltpu.VMEM((4, BLOCK, WIDTH), BF16),
        pltpu.VMEM((2, 8, 128), F32),
        pltpu.VMEM((128, 64), F32),
        pltpu.VMEM((2, 64, 64), BF16),
        pltpu.VMEM((256, 256), BF16),
        pltpu.VMEM((128, 128), BF16),
        pltpu.VMEM((256, 256), BF16),
        dma((5,)), dma((len(PARCELS) + 1,)),
        *[dma((2, PIECES))] * 4, dma((2,)),
        dma((len(PARCELS), 8)), dma((len(PARCELS), 8)), dma((4,)), dma((4,)),
        dma((4, 4)), dma((4, 4)), dma((4,)), dma((4,)),
    ]
    result = pl.pallas_call(
        kernel,
        out_shape=pltpu.VMEM((PATCH, BLOCK, WIDTH), BF16),
        in_specs=[any_spec] * 5 + [vmem_spec] * 2 + [smem_spec] * 3,
        out_specs=vmem_spec,
        scratch_shapes=scratch,
        compiler_params=pltpu.CompilerParams(
            collective_id=0, has_side_effects=True, vmem_limit_bytes=56 * 1024 * 1024
        ),
    )(
        x, w_time_qkv, w_time_out, w_space_qkv, w_space_out,
        ln_time, ln_space, band_lo, band_hi, valid,
    )
    return jnp.transpose(result, (1, 0, 2))


def solution(mesh):
    placed = (P("tm", "patch", None), P(), P(), P(), P(), P(), P(), P("tm"), P("tm"), P())
    return jax.shard_map(
        on_device, mesh=mesh, in_specs=placed, out_specs=P("tm", "patch", None), check_vma=False
    )
```

time: 64.6 us -> 63.9 us (0.989)
  Pallas kernels: 62.1 us -> 61.4 us
    pallas_call x1, Pallas kernels: 62.1 us -> 61.4 us  [on_device(): pl.pallas_call(kernel, out_shape=pltpu.VMEM((PATCH, BLOCK, WIDTH), BF16),...]
where the time goes in v3:
time: 63.9 us; the launch traced here: 63.8 us
  Pallas kernels  61.4 us (96%)
  between operations  1.31 us (2%)
  local copies, waits for them, and re-layouts  1.02 us (2%)
    pallas_call x1, Pallas kernels, on_device(): pl.pallas_call(kernel, out_shape=pltpu.VMEM((PATCH, BLOCK, WIDTH), BF16),...  61.4 us

profile of v3, /device:TPU:1, one launch (start us, length us, event | category | flops | bytes accessed | tf_op | source)
XLA Modules:
  0.0 63.8 jit_solution(936861631994559540)
XLA Ops:
  1.3 61.4 %shard_map.100 = bf16[49,16,768]{2,1,0:T(8,128)(2,1)S(1)} custom-call(bf16[49,16,768]{2,1,0:T(8,128)(2,1)} %bitcast.3, bf16[768,2304]{1,0:T(8,128)(2,1)} %wtq_hbm.1, bf16[768,768]{1,0:T(8,128)(2,1)} %wto_hbm.1, bf16[768,2304]{1,0:T(8,128)(2,1)} %wsq_hbm.1, bf16[768,768]{1,0:T(8,128)(2,1)} %wso_hbm.1, f32[768]{0:T(1024)} %gain_t.1, f32[768]{0:T(1024)} %gain_s.1, ...), custom_call_target="tpu_custom_call" | custom-call | tf_op jit(solution)/shard_map/pallas_call | solution.py:433
  62.7 1.0 %copy.12 = bf16[16,49,768]{2,0,1:T(8,128)(2,1)} copy(bf16[16,49,768]{2,0,1:T(8,128)(2,1)S(1)} %bitcast.2) | data formatting | bytes 2408448

commit v4 on v3

--- a/solution.py
+++ b/solution.py
@@ -48,7 +48,8 @@
 
 
 def kernel(
-    x_hbm, wtq_hbm, wto_hbm, wsq_hbm, wso_hbm, gain_t, gain_s, band_lo, band_hi, valid, out,
+    x_hbm, wtq_hbm, wto_hbm, wsq_hbm, wso_hbm, gt_hbm, gs_hbm, band_lo, band_hi, valid_hbm, out,
+    gain_t, gain_s, valid,
     wtq, wto, wsq, wso, x4, nrm, kv, qs, mix, snd, lft, recv, rcl, xs, nrm2, qkv, smix,
     om, ol, ret, rl, retl, biasb, bias, perm3, perm6, perm7, perm5,
     lsem, csem, psnd, prcv, rsnd, rrcv, bsem,
@@ -81,18 +82,16 @@
             device_id=device, device_id_type=MESH,
         )
 
+    small_copies = []
+    for i, (src, dst) in enumerate(((valid_hbm, valid), (gt_hbm, gain_t), (gs_hbm, gain_s))):
+        cp = pltpu.make_async_copy(src, dst, lsem.at[4 + i])
+        cp.start()
+        small_copies.append(cp)
     w_copies = []
     for i, (src, dst) in enumerate(((wtq_hbm, wtq), (wto_hbm, wto), (wsq_hbm, wsq), (wso_hbm, wso))):
-        cp = pltpu.make_async_copy(src, dst, lsem.at[1 + i])
+        cp = pltpu.make_async_copy(src, dst, lsem.at[i])
         cp.start()
         w_copies.append(cp)
-
-    left_ok = (band_lo[0] <= -1) & (tm >= 1) & (valid[jnp.maximum(tm - 1, 0)] == 1)
-    right_ok = (band_hi[0] >= 1) & (tm <= 2 * pairs - 2) & (valid[jnp.minimum(tm + 1, 2 * pairs - 1)] == 1)
-    left = jnp.where(left_ok, 0.0, NINF)
-    right = jnp.where(right_ok, 0.0, NINF)
-    row8 = lax.broadcasted_iota(jnp.int32, (8, 128), 0)
-    biasb[side] = jnp.where(row8 == 0, left, right)
 
     barrier = pltpu.get_barrier_semaphore()
     for k in range(1, 8):
@@ -118,9 +117,22 @@
             remote(x4.at[1, piece(c)], x4.at[3, piece(c)], rsnd.at[0, c], rrcv.at[0, c], before),
             remote(x4.at[2, piece(c)], x4.at[0, piece(c)], rsnd.at[1, c], rrcv.at[1, c], behind),
         ])
+    for c in range(4):
+        for cp in part[c]:
+            cp.start()
+    for cp in small_copies:
+        cp.wait()
+    lane = lax.broadcasted_iota(jnp.int32, (1, 2 * pairs), 1)
+    flags = valid[...].reshape(1, 2 * pairs).astype(F32)
+    left_flag = jnp.sum(jnp.where(lane == tm - 1, flags, 0.0), axis=-1, keepdims=True)
+    right_flag = jnp.sum(jnp.where(lane == tm + 1, flags, 0.0), axis=-1, keepdims=True)
+    left_ok = (band_lo[0] <= -1) & (left_flag == 1.0)
+    right_ok = (band_hi[0] >= 1) & (right_flag == 1.0)
+    row8 = lax.broadcasted_iota(jnp.int32, (8, 128), 0)
+    biasb[side] = jnp.where(row8 == 0, jnp.where(left_ok, 0.0, NINF), jnp.where(right_ok, 0.0, NINF))
     bias_copy = remote(biasb.at[side], biasb.at[side], bsem.at[0], bsem.at[1], partner)
     bias_copy.start()
-    for c in range(PIECES):
+    for c in range(4, PIECES):
         for cp in part[c]:
             cp.start()
 
@@ -393,10 +405,13 @@
 def on_device(frames_in, ln_time, w_time_qkv, w_time_out, ln_space, w_space_qkv, w_space_out, band_lo, band_hi, valid):
     x = jnp.transpose(frames_in, (1, 0, 2))
     any_spec = pl.BlockSpec(memory_space=pl.ANY)
+    smem_spec = pl.BlockSpec(memory_space=pltpu.SMEM)
     vmem_spec = pl.BlockSpec(memory_space=pltpu.VMEM)
-    smem_spec = pl.BlockSpec(memory_space=pltpu.SMEM)
     dma = pltpu.SemaphoreType.DMA
     scratch = [
+        pltpu.VMEM((WIDTH,), F32),
+        pltpu.VMEM((WIDTH,), F32),
+        pltpu.VMEM(valid.shape, jnp.int32),
         pltpu.VMEM((WIDTH, 3 * WIDTH), BF16),
         pltpu.VMEM((WIDTH, WIDTH), BF16),
         pltpu.VMEM((WIDTH, 3 * WIDTH), BF16),
@@ -425,7 +440,7 @@
         pltpu.VMEM((256, 256), BF16),
         pltpu.VMEM((128, 128), BF16),
         pltpu.VMEM((256, 256), BF16),
-        dma((5,)), dma((len(PARCELS) + 1,)),
+        dma((7,)), dma((len(PARCELS) + 1,)),
         *[dma((2, PIECES))] * 4, dma((2,)),
         dma((len(PARCELS), 8)), dma((len(PARCELS), 8)), dma((4,)), dma((4,)),
         dma((4, 4)), dma((4, 4)), dma((4,)), dma((4,)),
@@ -433,7 +448,7 @@
     result = pl.pallas_call(
         kernel,
         out_shape=pltpu.VMEM((PATCH, BLOCK, WIDTH), BF16),
-        in_specs=[any_spec] * 5 + [vmem_spec] * 2 + [smem_spec] * 3,
+        in_specs=[any_spec] * 7 + [smem_spec] * 2 + [any_spec],
         out_specs=vmem_spec,
         scratch_shapes=scratch,
         compiler_params=pltpu.CompilerParams(

time: 63.9 us -> 65.7 us (1.028)
  Pallas kernels: 61.4 us -> 63.3 us
    pallas_call x1, Pallas kernels: 61.4 us -> 63.3 us  [on_device(): pl.pallas_call(kernel, out_shape=pltpu.VMEM((PATCH, BLOCK, WIDTH), BF16),...]
where the time goes in v4:
time: 65.7 us; the launch traced here: 65.6 us
  Pallas kernels  63.3 us (96%)
  between operations  1.31 us (2%)
  local copies, waits for them, and re-layouts  1.02 us (2%)
    pallas_call x1, Pallas kernels, on_device(): pl.pallas_call(kernel, out_shape=pltpu.VMEM((PATCH, BLOCK, WIDTH), BF16),...  63.3 us

profile of v4, /device:TPU:1, one launch (start us, length us, event | category | flops | bytes accessed | tf_op | source)
XLA Modules:
  0.0 65.6 jit_solution(216120702099510277)
XLA Ops:
  1.3 63.3 %shard_map.100 = bf16[49,16,768]{2,1,0:T(8,128)(2,1)S(1)} custom-call(bf16[49,16,768]{2,1,0:T(8,128)(2,1)} %bitcast.3, bf16[768,2304]{1,0:T(8,128)(2,1)} %wtq_hbm.1, bf16[768,768]{1,0:T(8,128)(2,1)} %wto_hbm.1, bf16[768,2304]{1,0:T(8,128)(2,1)} %wsq_hbm.1, bf16[768,768]{1,0:T(8,128)(2,1)} %wso_hbm.1, f32[768]{0:T(1024)} %gt_hbm.1, f32[768]{0:T(1024)} %gs_hbm.1, ...), custom_call_target="tpu_custom_call" | custom-call | tf_op jit(solution)/shard_map/pallas_call | solution.py:448
  64.6 1.0 %copy.12 = bf16[16,49,768]{2,0,1:T(8,128)(2,1)} copy(bf16[16,49,768]{2,0,1:T(8,128)(2,1)S(1)} %bitcast.2) | data formatting | bytes 2408448
